TPU v7x, 256 devices: a whole 4x4x8 slice. The times are simulated.
256 devices in a mesh: gx: 8 (over x_lo, y), gy: 8 (over z), gz: 4 (over x_hi, core).
Axes of the slice: x: 4 (x_hi: 2, x_lo: 2; x = x_hi * 2 + x_lo), y: 4, z: 8, core: 2. Of those that a mesh axis runs over, the one named last changes fastest.
Arguments:
- out_grad: bfloat16 [4096, 16384], P('gx', ('gy', 'gz')), may hold values from -0.09375 to 0.09375
- layer_input: bfloat16 [4096, 16384], P('gx', ('gy', 'gz')), may hold values from -6 to 6
- out_weight: bfloat16 [16384, 16384], P(('gy', 'gz'), 'gx'), may hold values from -0.046875 to 0.046875
- saved_queries: bfloat16 [4096, 16384], P('gx', ('gy', 'gz'))
- saved_keys: bfloat16 [4096, 1024], P('gx')
- saved_values: bfloat16 [4096, 1024], P('gx'), may hold values from -6 to 6
- query_down: bfloat16 [16384, 32], P(('gy', 'gz')), may hold values from -0.046875 to 0.046875
- query_up: bfloat16 [32, 16384], P(None, ('gy', 'gz')), may hold values from -0.046875 to 0.046875
- value_down: bfloat16 [16384, 32], P(('gy', 'gz')), may hold values from -0.046875 to 0.046875
- value_up: bfloat16 [32, 1024], replicated, may hold values from -0.1875 to 0.1875
- lengths: int32 [8], P('gx'), may hold values from 128 to 512, as said below
Outputs:
- query_down_grad: float32 [16384, 32], P(('gy', 'gz'))
- query_up_grad: float32 [32, 16384], P(None, ('gy', 'gz'))
- value_down_grad: float32 [16384, 32], P(('gy', 'gz'))
- value_up_grad: float32 [32, 1024], replicated
Inputs may be any that keep to these rules, and one draw needn't show every extreme that they name: `lengths`: at least one sequence of each draw is full.
All inputs are finite; a program needn't handle non-finite values.
Results may differ from a plain program's by a relative error of at most 0.0042.
Values may be sent and summed in bfloat16 or wider, within the bound.
A program may use at most 128 MiB of HBM per device.

v0:
```python
import functools

import jax
import jax.numpy as jnp
from jax import lax
from jax.experimental import pallas as pl
from jax.experimental.pallas import tpu as pltpu
from jax.sharding import PartitionSpec as P

HQ = 128
KVH = 8
HD = 128
R = 32

adapter_scale = 2.0
mask_fill = -1e30
MESH = pl.DeviceIdType.MESH
ROWS = 8


def drain(ref, sem):
    pltpu.make_async_copy(ref, ref, sem).wait()


def send_to(src, dst, send_sem, recv_sem, device):
    return pltpu.make_async_remote_copy(
        src_ref=src,
        dst_ref=dst,
        send_sem=send_sem,
        recv_sem=recv_sem,
        device_id=device,
        device_id_type=MESH,
    )


def spread(count, me, device_of, src_of, dst, send_sem, recv_sem):
    pltpu.make_async_copy(src_of(me), dst, recv_sem).start()

    middle = count // 2

    def step(index, carry):
        offset = jnp.where(index < count - middle, middle + index, count - 1 - index)
        peer = lax.rem(me + offset, count)
        send_to(src_of(peer), dst, send_sem, recv_sem, device_of(peer)).start()
        return carry

    lax.fori_loop(0, count - 1, step, 0)


def greet(count, me, device_of):
    def step(offset, carry):
        peer = lax.rem(me + offset, count)
        pl.semaphore_signal(
            pltpu.get_barrier_semaphore(), inc=1, device_id=device_of(peer), device_id_type=MESH
        )
        return carry

    lax.fori_loop(1, count, step, 0)


def rows_of(index, count):
    return pl.ds(pl.multiple_of(index * count, count), count)


def grad_kernel(
    sizes,
    a_ref,
    w_ref,
    li_ref,
    query_ref,
    value_ref,
    out_ref,
    mid_ref,
    li_buf,
    dw_buf,
    t_buf,
    a_buf,
    w_buf,
    w_far,
    c_part,
    c_own,
    c_recv,
    x_send,
    x_recv,
    d_send,
    d_recv,
    mid_part,
    mid_recv,
    mid_sum,
    mid_all,
    t_sems,
    first_sems,
    w_sems,
    far_sems,
    twin_sems,
    ring_send,
    ring_recv,
    c_sems,
    c_arrived,
    x_sems,
    x_arrived,
    d_sems,
    m_sems,
    gate,
    in_sems,
    attend,
):
    gx, gy, gz = sizes
    col, lev, place = lax.axis_index("gx"), lax.axis_index("gy"), lax.axis_index("gz")
    far, core = place // 2, lax.rem(place, 2)
    sides = gx // 2
    near_x, side = col // sides, lax.rem(col, sides)
    slots = gy * gz
    slot_me = lev * gz + place
    seq, width = a_ref.shape
    heads = w_ref.shape[0]
    unit = seq // slots
    chunk = unit * gz
    last = gy // 2

    def slot_device(index):
        return (col, index // gz, lax.rem(index, gz))

    def plane_device(index):
        return (index // gz, lev, lax.rem(index, gz))

    copies = [
        pltpu.make_async_copy(li_ref, li_buf, in_sems.at[0]),
        pltpu.make_async_copy(query_ref, dw_buf.at[0, :R], in_sems.at[1]),
        pltpu.make_async_copy(value_ref, dw_buf.at[0, R : 2 * R], in_sems.at[2]),
        pltpu.make_async_copy(query_ref, dw_buf.at[1, 2 * R : 3 * R], in_sems.at[3]),
        pltpu.make_async_copy(value_ref, dw_buf.at[1, 3 * R :], in_sems.at[4]),
    ]
    for copy in copies:
        copy.start()
    none = jnp.zeros((2 * R, width), jnp.bfloat16)
    dw_buf[0, 2 * R :] = none
    dw_buf[1, : 2 * R] = none

    greet(slots, slot_me, slot_device)
    greet(gx * gz, col * gz + place, plane_device)

    pl.semaphore_wait(pltpu.get_barrier_semaphore(), slots - 1 + gx * gz - 1)

    def level_send(away):
        other = lax.rem(lev + away, gy)
        return send_to(
            a_ref.at[rows_of(other, chunk)],
            t_buf.at[lev],
            t_sems.at[0, away],
            t_sems.at[1, away],
            (col, other, place),
        )

    order = [last]
    for away in range(last - 1, 0, -1):
        order += [away, gy - away]
    for away in order:
        level_send(away).start()

    def column_send(to, block):
        def one(index, carry):
            at = lax.rem(place + index, gz)
            source = block.at[rows_of(at, unit)]
            target = a_buf.at[place, 0, rows_of(side * 2 + near_x, unit)]
            mine = jnp.logical_and(col == to, at == place)

            @pl.when(mine)
            def _():
                pltpu.make_async_copy(source, target, first_sems.at[1]).start()

            @pl.when(jnp.logical_not(mine))
            def _():
                send_to(
                    source, target, first_sems.at[0], first_sems.at[1], (to, lev, at)
                ).start()

            return carry

        lax.fori_loop(0, gz, one, 0)

    column_send(lev, a_ref.at[rows_of(lev, chunk)])

    sibling = (col, lev, far * 2 + 1 - core)
    opposite = (col, lev, (1 - far) * 2 + core)
    shares = 4
    band = heads // shares
    own_w = pltpu.make_async_copy(w_ref, w_buf.at[0], w_sems.at[0])
    own_w.start()
    twin_w = send_to(w_ref, w_buf.at[1], w_sems.at[1], w_sems.at[2], sibling)
    twin_w.start()

    def far_w(share):
        return send_to(
            w_ref.at[pl.ds(share * band, band)],
            w_far.at[share, 0],
            far_sems.at[0, share],
            far_sems.at[1, share],
            opposite,
        )

    def pass_w(share):
        return send_to(
            w_far.at[share, 0],
            w_far.at[share, 1],
            twin_sems.at[0, share],
            twin_sems.at[1, share],
            sibling,
        )

    far_w(0).start()

    for away in order:
        other = lax.rem(lev + gy - away, gy)
        level_send(away).wait_recv()
        column_send(other, t_buf.at[other])

    up = (col, lax.rem(lev + 1, gy), place)
    down = (col, lax.rem(lev + gy - 1, gy), place)

    def ring(way, hop, which):
        parts = slice(2 * which, 2 * which + 2)
        start = 2 * hop - 3 + way if hop > 1 else 0
        end = 2 * hop - 1 + (way if hop < last else 0)
        index = 2 * (hop - 1) + (which if hop < last else 0)
        return send_to(
            a_buf.at[parts, start],
            a_buf.at[parts, end],
            ring_send.at[way, index],
            ring_recv.at[way, index],
            (up, down)[way],
        )

    cut = gy - 2

    def products(start, steps, weights):
        total = jnp.zeros((steps * gx * unit, weights(0).shape[0]), jnp.float32)
        for part in range(gz):
            total += lax.dot_general(
                a_buf[part, start : start + steps].reshape(steps * gx * unit, width),
                weights(part),
                (((1,), (1,)), ((), ())),
                preferred_element_type=jnp.float32,
            )
        return total

    def keep(block, start, steps, columns, total):
        total = total.reshape(steps, sides, 2, unit, total.shape[1])
        c_part[block, start : start + steps, :, :, :, columns] = total.astype(jnp.bfloat16)
        for way in range(sides):

            @pl.when(side == way)
            def _():
                c_own[block, start : start + steps, :, :, columns] = total[:, way]

    def give(blocks, start, steps, columns, kind):
        for at, end, group in (
            (start, min(start + steps, cut), kind),
            (max(start, cut), start + steps, 1),
        ):
            if end > at:
                for away in range(1, sides):
                    other = lax.rem(side + away, sides)
                    send_to(
                        c_part.at[blocks, at:end, other, :, :, columns],
                        c_recv.at[away - 1, blocks, at:end, :, :, columns],
                        c_sems.at[0],
                        c_arrived.at[group],
                        (near_x * sides + other, lev, place),
                    ).start()

    def near(start, steps):
        def one_block(block, carry):
            total = products(
                start, steps, lambda part: w_buf[block, :, part * width : (part + 1) * width]
            )
            keep(block, start, steps, slice(0, heads), total)
            give(pl.ds(block, 1), start, steps, slice(0, heads), 0)
            return carry

        lax.fori_loop(0, 2, one_block, 0)

    def far_part(start, share):
        total = products(
            start,
            2,
            lambda part: w_far[share, :, :, part * width : (part + 1) * width].reshape(
                2 * band, width
            ),
        )
        columns = slice(share * band, (share + 1) * band)
        for index in range(2):
            keep(2 + index, start, 2, columns, total[:, index * band : (index + 1) * band])
        give(slice(2, 4), start, 2, columns, 2)

    drain(a_buf.at[: gz - 1, 0], first_sems.at[0])
    drain(a_buf.at[gz - 1, 0, : (gx - 1) * unit], first_sems.at[0])

    def gate_signal(offset, carry):
        peer = lax.rem(near_x * gz + place + offset, 2 * gz)
        pl.semaphore_signal(
            gate,
            inc=1,
            device_id=(peer // gz * sides + side, lev, lax.rem(peer, gz)),
            device_id_type=MESH,
        )
        return carry

    lax.fori_loop(1, 2 * gz, gate_signal, 0)
    attend(0)
    pl.semaphore_wait(gate, 2 * gz - 1)
    far_w(1).start()
    far_w(2).start()
    far_w(3).start()
    drain(a_buf.at[:, 0], first_sems.at[1])
    for which in range(2):
        for way in range(2):
            ring(way, 1, which).start()
    packed = seq // 2
    for copy in copies:
        copy.wait()
    lanes = (((1,), (1,)), ((), ()))
    mid_part[...] = lax.dot_general(
        li_buf[:packed, :], dw_buf[0], lanes, preferred_element_type=jnp.float32
    ) + lax.dot_general(li_buf[packed:, :], dw_buf[1], lanes, preferred_element_type=jnp.float32)

    piece = packed // slots
    spread(
        slots,
        slot_me,
        slot_device,
        lambda index: mid_part.at[rows_of(index, piece)],
        mid_recv.at[slot_me],
        m_sems.at[0],
        m_sems.at[1],
    )

    own_w.wait()
    twin_w.wait_recv()
    near(0, 1)
    attend(1)
    far_w(0).wait_recv()
    pass_w(0).start()
    for hop in range(1, last):
        for which in range(2):
            for way in range(2):
                ring(way, hop, which).wait_recv()
                if hop < last - 1 or way == which:
                    ring(way, hop + 1, which).start()
        near(2 * hop - 1, 2)
        if hop < last - 1:
            attend(hop + 1)
        if hop == 1:
            pass_w(0).wait_recv()
        for share in range(hop):
            far_part(2 * hop - 2, share)
        for share in [hop] if hop < last - 1 else range(hop, shares):
            far_w(share).wait_recv()
            pass_w(share).start()
            far_w(share).wait_send()
            pass_w(share).wait_recv()
            for start in range(0, 2 * hop, 2):
                far_part(start, share)
        if hop == max(1, last - 2):
            drain(mid_recv, m_sems.at[1])
            mid_sum[...] = jnp.sum(mid_recv[...], axis=0)
            spread(
                slots,
                slot_me,
                slot_device,
                lambda index: mid_sum,
                mid_all.at[rows_of(slot_me, piece)],
                m_sems.at[2],
                m_sems.at[3],
            )
    ring(0, last, 0).wait_recv()
    ring(1, last, 1).wait_recv()
    near(gy - 1, 1)
    for share in range(shares):
        far_part(gy - 2, share)

    def hand_over(low, high, start, end, group):
        drain(c_recv.at[:, low:high, start:end], c_arrived.at[group])

        def one(block, carry):
            total = c_own[block, start:end]
            for away in range(sides - 1):
                total += c_recv[away, block, start:end].astype(jnp.float32)
            for half in range(2):

                @pl.when(near_x == half)
                def _():
                    x_send[block, start:end] = total[:, 1 - half].astype(jnp.bfloat16)
                    c_own[block, start:end, 0] = total[:, half]

            return carry

        lax.fori_loop(low, high, one, 0)
        send_to(
            x_send.at[low:high, start:end],
            x_recv.at[low:high, start:end],
            x_sems.at[group],
            x_arrived.at[group],
            ((1 - near_x) * sides + side, lev, place),
        ).start()

    def hand_out(low, high, start, end, group):
        drain(x_recv.at[low:high, start:end], x_arrived.at[group])

        def one(block, carry):
            total = c_own[block, start:end, 0] + x_recv[block, start:end].astype(jnp.float32)
            d_send[block, start:end] = total.astype(jnp.bfloat16)
            return carry

        lax.fori_loop(low, high, one, 0)
        for block in range(low, high):
            if block == 0:
                d_recv[place, start:end] = d_send[0, start:end]
                continue
            at = (far if block < 2 else 1 - far) * 2 + (1 - core if block % 2 else core)
            send_to(
                d_send.at[block, start:end],
                d_recv.at[place, start:end],
                d_sems.at[0],
                d_sems.at[1],
                (col, lev, at),
            ).start()

    hand_over(0, 2, 0, cut, 0)
    hand_over(2, 4, 0, cut, 2)
    hand_out(0, 2, 0, cut, 0)
    hand_over(0, 4, cut, gy, 1)
    hand_out(2, 4, 0, cut, 2)
    hand_out(0, 4, cut, gy, 1)

    for away in order:
        level_send(away).wait_send()
    twin_w.wait_send()
    far_w(0).wait_send()
    for share in range(shares):
        pass_w(share).wait_send()
    for hop in range(1, last + 1):
        for which in range(2):
            for way in range(2):
                if hop < last or way == which:
                    ring(way, hop, which).wait_send()
    drain(mid_recv.at[: slots - 1], m_sems.at[0])
    drain(mid_recv.at[: slots - 1], m_sems.at[2])
    drain(mid_all, m_sems.at[3])
    mid_ref[...] = mid_all[...]
    drain(c_part.at[:, : gy * (sides - 1) // sides], c_sems.at[0])
    drain(x_send.at[:2, :cut], x_sems.at[0])
    drain(x_send.at[:, cut:], x_sems.at[1])
    drain(x_send.at[2:, :cut], x_sems.at[2])
    drain(d_send.at[1:], d_sems.at[0])
    drain(d_send.at[1:], d_sems.at[1])

    for start in range(gy):
        hop = (start + 1) // 2
        level = lax.rem(lev + (gy - hop if start % 2 else hop), gy)

        def one_place(at, carry):
            out_ref[rows_of(level * gz + at, unit), :] = d_recv[at, start]
            return carry

        lax.fori_loop(0, gz, one_place, 0)


def split_low(array):
    high = array.astype(jnp.bfloat16)
    return high, (array - high.astype(jnp.float32)).astype(jnp.bfloat16)


def product(left, right, left_dim, right_dim):
    return lax.dot_general(
        left, right, (((left_dim,), (right_dim,)), ((), ())), preferred_element_type=jnp.float32
    )


def attention_kernel(
    lengths_ref,
    queries_ref,
    keys_ref,
    attention_ref,
    head,
):
    seq = queries_ref.shape[0]
    packed = seq // 2
    length = lengths_ref[0]
    columns = pl.ds(pl.multiple_of(head * HD, HD), HD)
    for block in range(2):
        rows = slice(block * packed, (block + 1) * packed)
        span = (block + 1) * packed
        shape = (packed, span)
        row = lax.broadcasted_iota(jnp.int32, shape, 0) + block * packed
        key = lax.broadcasted_iota(jnp.int32, shape, 1)
        scores = product(queries_ref[rows, columns], keys_ref[:span], 1, 1) * HD ** (-0.5)
        scores = jnp.where((key <= row) & (key < length), scores, mask_fill)
        raised = jnp.exp(scores - jnp.max(scores, axis=1, keepdims=True))
        attention_ref[head, rows, :span] = raised / jnp.sum(raised, axis=1, keepdims=True)


def sum_kernel(
    sizes,
    lengths_ref,
    out_ref,
    li_ref,
    grad_ref,
    mid_ref,
    keys_ref,
    values_ref,
    up_ref,
    value_up_ref,
    attention_ref,
    query_grad,
    value_grad,
    factor_ref,
    raise_ref,
    value_ref,
    factor_recv,
    factor_sum,
    factor_all,
    raise_recv,
    raise_sum,
    raise_all,
    value_recv,
    value_sum,
    value_plane,
    value_done,
    value_level,
    value_all,
    down_part,
    down_recv,
    down_sum,
    down_all,
    sends,
    recvs,
):
    gx, gy, gz = sizes
    col, lev, place = lax.axis_index("gx"), lax.axis_index("gy"), lax.axis_index("gz")
    slots = gy * gz
    slot_me = lev * gz + place
    seq, width = query_grad.shape
    packed = seq // 2
    length = lengths_ref[0]

    def slot_device(index):
        return (col, index // gz, lax.rem(index, gz))

    def column_device(index):
        return (index, lev, place)

    def level_device(index):
        return (col, index, place)

    def place_device(index):
        return (col, lev, index)

    value_grad[...] = jnp.zeros_like(value_grad)

    def one_head(head, carry):
        columns = pl.ds(pl.multiple_of(head * HD, HD), HD)
        for block in range(2):
            rows = slice(block * packed, (block + 1) * packed)
            span = (block + 1) * packed
            attention = attention_ref[head, rows, :span]
            grads = grad_ref[rows, columns]
            line = lax.broadcasted_iota(jnp.int32, grads.shape, 0) + block * packed
            grads = jnp.where(line < length, grads.astype(jnp.float32), 0.0).astype(jnp.bfloat16)
            value_grad[:span] += product(attention.astype(jnp.bfloat16), grads, 0, 0)
            prob_grad = product(grads, values_ref[:span], 1, 1)
            centre = jnp.sum(attention * prob_grad, axis=1, keepdims=True)
            score_grad = (attention * (prob_grad - centre)).astype(jnp.bfloat16)
            query_grad[rows, columns] = product(score_grad, keys_ref[:span], 1, 0) * HD ** (-0.5)
        return carry

    lax.fori_loop(0, width // HD, one_head, 0)

    total = jnp.zeros((packed, 128), jnp.float32)
    raised = jnp.zeros((R, width), jnp.float32)
    value_part = jnp.zeros((R, HD), jnp.float32)
    mid_high, mid_low = split_low(mid_ref[...])
    for block in range(2):
        rows = slice(block * packed, (block + 1) * packed)
        high, low = split_low(query_grad[rows])
        total += product(high, up_ref[block], 1, 1) + product(low, up_ref[block], 1, 1)
        every = product(mid_high, high, 0, 0) + product(mid_low, high, 0, 0)
        every += product(mid_high, low, 0, 0)
        raised += every[block * 2 * R : block * 2 * R + R]
        high, low = split_low(value_grad[rows])
        total += product(high, value_up_ref[block], 1, 1)
        total += product(low, value_up_ref[block], 1, 1)
        every = product(mid_high, high, 0, 0) + product(mid_low, high, 0, 0)
        every += product(mid_high, low, 0, 0)
        value_part += every[block * 2 * R + R : (block + 1) * 2 * R]
    factor_ref[...] = total.reshape(factor_ref.shape)
    raised = adapter_scale * raised
    value_part = adapter_scale * value_part
    raise_ref[...] = jnp.concatenate(
        [raised[:, at : at + 128] for at in range(0, width, 128)], axis=0
    ).reshape(raise_ref.shape)
    per = R // gx
    value_ref[...] = jnp.zeros_like(value_ref)
    for at in range(gx):
        value_ref[at, :per] = value_part[at * per : (at + 1) * per]

    spread(slots, slot_me, slot_device, lambda i: factor_ref.at[i], factor_recv.at[slot_me], sends.at[0], recvs.at[0])
    spread(gx, col, column_device, lambda i: value_ref.at[i], value_recv.at[col], sends.at[1], recvs.at[1])
    spread(gx, col, column_device, lambda i: raise_ref.at[i], raise_recv.at[col], sends.at[2], recvs.at[2])

    drain(factor_recv, recvs.at[0])
    factor_sum[...] = jnp.sum(factor_recv[...], axis=0)
    spread(slots, slot_me, slot_device, lambda i: factor_sum, factor_all.at[slot_me], sends.at[3], recvs.at[3])
    drain(value_recv, recvs.at[1])
    value_sum[...] = jnp.sum(value_recv[...], axis=0)
    spread(gz, place, place_device, lambda i: value_sum, value_plane.at[place], sends.at[4], recvs.at[4])
    drain(raise_recv, recvs.at[2])
    raise_sum[...] = jnp.sum(raise_recv[...], axis=0)
    spread(gx, col, column_device, lambda i: raise_sum, raise_all.at[col], sends.at[5], recvs.at[5])

    drain(factor_all, recvs.at[3])
    factor = factor_all[...].reshape(packed, 128)
    factor_high, factor_low = split_low(factor)

    def project(rows):
        block = li_ref[rows, :]
        dims = (((0,), (0,)), ((), ()))
        return lax.dot_general(
            block, factor_high, dims, preferred_element_type=jnp.float32
        ) + lax.dot_general(block, factor_low, dims, preferred_element_type=jnp.float32)

    first = project(slice(0, packed))
    second = project(slice(packed, 2 * packed))
    lane = lax.broadcasted_iota(jnp.int32, first.shape, 1)
    both = adapter_scale * jnp.where(lane < 64, first, second)
    both = both + pltpu.roll(both, 64, 1)
    rows = both.shape[0] // 2
    both = jnp.where(lane[:rows] < 64, both[:rows], both[rows:])
    down_part[...] = both.reshape(down_part.shape)
    spread(gx, col, column_device, lambda i: down_part.at[i], down_recv.at[col], sends.at[6], recvs.at[6])

    drain(value_plane, recvs.at[4])
    value_done[...] = jnp.sum(value_plane[...], axis=0)
    spread(gy, lev, level_device, lambda i: value_done, value_level.at[lev], sends.at[7], recvs.at[7])
    drain(value_level, recvs.at[7])
    spread(gx, col, column_device, lambda i: value_level, value_all.at[col], sends.at[8], recvs.at[8])

    drain(down_recv, recvs.at[6])
    down_sum[...] = jnp.sum(down_recv[...], axis=0)
    spread(gx, col, column_device, lambda i: down_sum, down_all.at[col], sends.at[9], recvs.at[9])

    drain(raise_all, recvs.at[5])
    raised = raise_all[...].reshape(-1, 128)
    for at in range(raised.shape[0] // R):
        out_ref[:, at * 128 : (at + 1) * 128] = raised[at * R : (at + 1) * R]
    drain(value_all, recvs.at[8])
    for at in range(gx):
        for level in range(gy):
            start = width + 2 * li_ref.shape[1] + level * 128
            out_ref[at * per : (at + 1) * per, start : start + 128] = value_all[at, level, :per]
    drain(down_all, recvs.at[9])
    turned = down_all[...].reshape(-1, 128).T
    for at, source in enumerate((0, 2, 1, 3)):
        start = width + at * rows
        out_ref[:, start : start + rows] = turned[source * R : (source + 1) * R]
    drain(factor_recv.at[: slots - 1], sends.at[0])
    drain(value_recv.at[: gx - 1], sends.at[1])
    drain(raise_recv.at[: gx - 1], sends.at[2])
    drain(factor_all.at[: slots - 1], sends.at[3])
    drain(value_plane.at[: gz - 1], sends.at[4])
    drain(raise_all.at[: gx - 1], sends.at[5])
    drain(down_recv.at[: gx - 1], sends.at[6])
    drain(value_level.at[: gy - 1], sends.at[7])
    drain(value_all.at[: gx - 1], sends.at[8])
    drain(down_all.at[: gx - 1], sends.at[9])


def whole_kernel(
    sizes,
    counts,
    lengths_ref,
    a_ref,
    w_ref,
    li_any,
    query_down_any,
    value_down_any,
    queries_any,
    keys_any,
    values_any,
    up_any,
    value_up_any,
    out_ref,
    *scratch,
):
    gx, gy, gz = sizes
    first, second = scratch[: counts[0]], scratch[counts[0] : counts[0] + counts[1]]
    grad_ref, mid_ref, queries_ref, keys_ref, values_ref = second[:5]
    up_ref, value_up_ref, attention_ref = second[5:8]
    in_sems = scratch[-1]
    seq, width = queries_any.shape
    kv = (lax.axis_index("gy") * gz + lax.axis_index("gz")) * (width // HD) // (HQ // KVH)
    kv_columns = pl.ds(pl.multiple_of(kv * HD, HD), HD)
    copies = [
        pltpu.make_async_copy(queries_any, queries_ref, in_sems.at[0]),
        pltpu.make_async_copy(keys_any.at[:, kv_columns], keys_ref, in_sems.at[1]),
        pltpu.make_async_copy(values_any.at[:, kv_columns], values_ref, in_sems.at[2]),
        pltpu.make_async_copy(up_any, up_ref.at[0, :R], in_sems.at[3]),
        pltpu.make_async_copy(up_any, up_ref.at[1, 2 * R : 3 * R], in_sems.at[4]),
        pltpu.make_async_copy(
            value_up_any.at[:, kv_columns], value_up_ref.at[0, R : 2 * R], in_sems.at[5]
        ),
        pltpu.make_async_copy(
            value_up_any.at[:, kv_columns], value_up_ref.at[1, 3 * R :], in_sems.at[6]
        ),
    ]

    def attend(step):
        if step == 0:
            up_ref[0, R:] = jnp.zeros((3 * R, width), jnp.bfloat16)
            up_ref[1, : 2 * R] = jnp.zeros((2 * R, width), jnp.bfloat16)
            up_ref[1, 3 * R :] = jnp.zeros((R, width), jnp.bfloat16)
            value_up_ref[0, :R] = jnp.zeros((R, HD), jnp.bfloat16)
            value_up_ref[0, 2 * R :] = jnp.zeros((2 * R, HD), jnp.bfloat16)
            value_up_ref[1, : 3 * R] = jnp.zeros((3 * R, HD), jnp.bfloat16)
            for copy in copies:
                copy.wait()
        steps = gy // 2
        heads = width // HD

        def one(head, carry):
            attention_kernel(lengths_ref, queries_ref, keys_ref, attention_ref, head)
            return carry

        lax.fori_loop(step * heads // steps, (step + 1) * heads // steps, one, 0)

    for copy in copies:
        copy.start()
    grad_kernel(
        sizes,
        a_ref,
        w_ref,
        li_any,
        query_down_any,
        value_down_any,
        grad_ref,
        mid_ref,
        *first,
        attend,
    )
    sum_kernel(
        sizes,
        lengths_ref,
        out_ref,
        first[0],
        grad_ref,
        mid_ref,
        keys_ref,
        values_ref,
        up_ref,
        value_up_ref,
        attention_ref,
        *second[8:],
    )


def part_kernel(whole_ref, *part_refs):
    start = 0
    for part_ref in part_refs:
        part_ref[...] = whole_ref[:, start : start + part_ref.shape[1]]
        start += part_ref.shape[1]


def body(
    sizes,
    out_grad,
    layer_input,
    out_weight,
    saved_queries,
    saved_keys,
    saved_values,
    query_down,
    query_up,
    value_down,
    value_up,
    lengths,
):
    gx, gy, gz = sizes
    seq, width = out_grad.shape
    heads, depth = out_weight.shape
    slots = gy * gz
    unit = seq // slots
    piece = seq // 2 // slots
    sides = gx // 2
    single, low = jnp.float32, jnp.bfloat16
    dma = pltpu.SemaphoreType.DMA
    first = [
        pltpu.VMEM((seq, width), low),
        pltpu.VMEM((2, 4 * R, width), low),
        pltpu.VMEM((gy, unit * gz, width), low),
        pltpu.VMEM((gz, gy, gx * unit, width), low),
        pltpu.VMEM((2, heads, depth), low),
        pltpu.VMEM((4, 2, heads // 4, depth), low),
        pltpu.VMEM((gz, gy, sides, 2, unit, heads), low),
        pltpu.VMEM((gz, gy, 2, unit, heads), single),
        pltpu.VMEM((sides - 1, gz, gy, 2, unit, heads), low),
        pltpu.VMEM((gz, gy, unit, heads), low),
        pltpu.VMEM((gz, gy, unit, heads), low),
        pltpu.VMEM((gz, gy, unit, heads), low),
        pltpu.VMEM((gz, gy, unit, heads), low),
        pltpu.VMEM((seq // 2, 128), single),
        pltpu.VMEM((slots, piece, 128), single),
        pltpu.VMEM((piece, 128), single),
        pltpu.VMEM((seq // 2, 128), single),
        dma((2, gy)),
        dma((2,)),
        dma((3,)),
        dma((2, 4)),
        dma((2, 4)),
        dma((2, gy - 1)),
        dma((2, gy - 1)),
        dma((1,)),
        dma((3,)),
        dma((3,)),
        dma((3,)),
        dma((2,)),
        dma((4,)),
        pltpu.SemaphoreType.REGULAR,
        dma((5,)),
    ]
    factor = (slots, piece, 128)
    raised = (gx, R * heads // 128 // gx, 128)
    value = (gx, max(ROWS, R // gx), 128)
    down = (gx, width // gx // 2, 128)
    shapes = [
        ((seq, heads), low),
        ((seq // 2, 128), single),
        ((seq, heads), low),
        ((seq, HD), low),
        ((seq, HD), low),
        ((2, 4 * R, heads), low),
        ((2, 4 * R, HD), low),
        ((heads // HD, seq, seq), single),
        ((seq, heads), single),
        ((seq, HD), single),
        (factor, single),
        (raised, single),
        (value, single),
        (factor, single),
        (factor[1:], single),
        (factor, single),
        (raised, single),
        (raised[1:], single),
        (raised, single),
        (value, single),
        (value[1:], single),
        ((gz,) + value[1:], single),
        (value[1:], single),
        ((gy,) + value[1:], single),
        ((gx, gy) + value[1:], single),
        (down, single),
        (down, single),
        (down[1:], single),
        (down, single),
    ]
    second = [pltpu.VMEM(shape, kind) for shape, kind in shapes] + [dma((10,)), dma((10,))]
    result = pl.pallas_call(
        functools.partial(whole_kernel, sizes, (len(first), len(second))),
        out_shape=jax.ShapeDtypeStruct((R, heads + 2 * width + gy * 128), single),
        in_specs=[pl.BlockSpec(memory_space=pltpu.SMEM)]
        + [pl.BlockSpec(memory_space=pl.ANY)] * 10,
        out_specs=pl.BlockSpec(memory_space=pltpu.VMEM),
        scratch_shapes=first + second + [dma((7,))],
        compiler_params=pltpu.CompilerParams(
            collective_id=0, has_side_effects=True, vmem_limit_bytes=60 << 20
        ),
        cost_estimate=pl.CostEstimate(
            flops=2 * seq * heads * depth * gx, bytes_accessed=16 << 20, transcendentals=0
        ),
    )(
        lengths,
        out_grad,
        out_weight,
        layer_input,
        query_down.T,
        value_down.T,
        saved_queries,
        saved_keys,
        saved_values,
        query_up,
        value_up,
    )
    parts = pl.pallas_call(
        part_kernel,
        out_shape=tuple(
            jax.ShapeDtypeStruct((R, count), single) for count in (heads, width, width, gy * 128)
        ),
    )(result)
    return (parts[1].T, parts[0], parts[2].T, parts[3])


def solution(mesh):
    sizes = tuple(mesh.shape[name] for name in ("gx", "gy", "gz"))
    return jax.shard_map(
        functools.partial(body, sizes),
        mesh=mesh,
        in_specs=(
            P("gx", ("gy", "gz")),
            P("gx", ("gy", "gz")),
            P(("gy", "gz"), "gx"),
            P("gx", ("gy", "gz")),
            P("gx", None),
            P("gx", None),
            P(("gy", "gz"), None),
            P(None, ("gy", "gz")),
            P(("gy", "gz"), None),
            P(),
            P("gx"),
        ),
        out_specs=(P(("gy", "gz"), None), P(None, ("gy", "gz")), P(("gy", "gz"), None), P()),
        check_vma=False,
    )
```

profile of v0, /device:TPU:4, one launch (start us, length us, event | category | flops | bytes accessed | tf_op | source)
XLA Modules:
  0.0 142.4 jit_solution(13197157415489134978)
XLA Ops:
  1.3 139.4 %shard_map.138.whole_ref = f32[32,2560]{1,0:T(8,128)} custom-call(s32[1]{0:T(128)S(6)} %copy.15.lengths_ref, bf16[512,512]{1,0:T(8,128)(2,1)} %a_ref.1, bf16[512,2048]{1,0:T(8,128)(2,1)} %w_ref.1, bf16[512,512]{1,0:T(8,128)(2,1)} %li_any.1, bf16[32,512]{1,0:T(8,128)(2,1)} %bitcast.6, bf16[32,512]{1,0:T(8,128)(2,1)} %bitcast.7, bf16[512,512]{1,0:T(8,128)(2,1)} %queries_any.1, ...), custom_call_target="tpu_custom_call" | custom-call | flops 8589934592 | bytes 16777216 | tf_op jit(solution)/shard_map/pallas_call | solution.py:866
  140.7 1.7 %shard_map.139 = (f32[32,512]{1,0:T(8,128)}, f32[32,512]{1,0:T(8,128)}, f32[32,512]{1,0:T(8,128)}, f32[32,1024]{1,0:T(8,128)}) custom-call(f32[32,2560]{1,0:T(8,128)} %shard_map.138.whole_ref), custom_call_target="tpu_custom_call" | custom-call | tf_op jit(solution)/shard_map/pallas_call | solution.py:892
where the time goes:
time: 143 us; the launch traced here: 142 us
  Pallas kernels  141 us (99%)
    pallas_call x1, Pallas kernels, body(): pl.pallas_call(functools.partial(whole_kernel, sizes, (len(first), len(se...  139 us

commit v1 on v0

--- a/solution.py
+++ b/solution.py
@@ -618,6 +618,10 @@
     raise_sum[...] = jnp.sum(raise_recv[...], axis=0)
     spread(gx, col, column_device, lambda i: raise_sum, raise_all.at[col], sends.at[5], recvs.at[5])
 
+    drain(value_plane, recvs.at[4])
+    value_done[...] = jnp.sum(value_plane[...], axis=0)
+    spread(gy, lev, level_device, lambda i: value_done, value_level.at[lev], sends.at[7], recvs.at[7])
+
     drain(factor_all, recvs.at[3])
     factor = factor_all[...].reshape(packed, 128)
     factor_high, factor_low = split_low(factor)
@@ -639,9 +643,6 @@
     down_part[...] = both.reshape(down_part.shape)
     spread(gx, col, column_device, lambda i: down_part.at[i], down_recv.at[col], sends.at[6], recvs.at[6])
 
-    drain(value_plane, recvs.at[4])
-    value_done[...] = jnp.sum(value_plane[...], axis=0)
-    spread(gy, lev, level_device, lambda i: value_done, value_level.at[lev], sends.at[7], recvs.at[7])
     drain(value_level, recvs.at[7])
     spread(gx, col, column_device, lambda i: value_level, value_all.at[col], sends.at[8], recvs.at[8])
 

time: 143 us -> 141 us (0.986)
  Pallas kernels: 141 us -> 138 us
    pallas_call x1, Pallas kernels: 139 us -> 137 us  [body(): pl.pallas_call(functools.partial(whole_kernel, sizes, (len(first), len(se...]
where the time goes in v1:
time: 141 us; the launch traced here: 140 us
  Pallas kernels  138 us (98%)
    pallas_call x1, Pallas kernels, body(): pl.pallas_call(functools.partial(whole_kernel, sizes, (len(first), len(se...  137 us

profile of v1, /device:TPU:4, one launch (start us, length us, event | category | flops | bytes accessed | tf_op | source)
XLA Modules:
  0.0 139.6 jit_solution(18222067175468123712)
XLA Ops:
  1.3 136.7 %shard_map.138.whole_ref = f32[32,2560]{1,0:T(8,128)} custom-call(s32[1]{0:T(128)S(6)} %copy.15.lengths_ref, bf16[512,512]{1,0:T(8,128)(2,1)} %a_ref.1, bf16[512,2048]{1,0:T(8,128)(2,1)} %w_ref.1, bf16[512,512]{1,0:T(8,128)(2,1)} %li_any.1, bf16[32,512]{1,0:T(8,128)(2,1)} %bitcast.6, bf16[32,512]{1,0:T(8,128)(2,1)} %bitcast.7, bf16[512,512]{1,0:T(8,128)(2,1)} %queries_any.1, ...), custom_call_target="tpu_custom_call" | custom-call | flops 8589934592 | bytes 16777216 | tf_op jit(solution)/shard_map/pallas_call | solution.py:867
  137.9 1.7 %shard_map.139 = (f32[32,512]{1,0:T(8,128)}, f32[32,512]{1,0:T(8,128)}, f32[32,512]{1,0:T(8,128)}, f32[32,1024]{1,0:T(8,128)}) custom-call(f32[32,2560]{1,0:T(8,128)} %shard_map.138.whole_ref), custom_call_target="tpu_custom_call" | custom-call | tf_op jit(solution)/shard_map/pallas_call | solution.py:893
